TPU v7x, 32 devices: a whole 2x2x4 slice. The times are simulated.
32 devices in a mesh: row: 8 (over z, x), col: 4 (over y, core).
Axes of the slice: x: 2, y: 2, z: 4, core: 2. Of those that a mesh axis runs over, the one named last changes fastest.
Arguments:
- image_emb: bfloat16 [128, 4, 1024], P('row', 'col'), may hold values from -16 to 16
- text_emb: bfloat16 [64, 8, 1024], P('col', 'row'), may hold values from -16 to 16
- logit_scale: float32 [1], replicated, may hold values from 2.5 to 5
Outputs:
- loss: float32 [], replicated
- image_grad: float32 [128, 4, 1024], P('row', 'col')
- text_grad: float32 [64, 8, 1024], P('col', 'row')
All inputs are finite; a program needn't handle non-finite values.
Results may differ from a plain program's by a relative error of at most 0.0075.
Values may be sent and summed in bfloat16 or wider, within the bound.
A program may use at most 64 MiB of HBM per device.

v0:
```python
import jax
import jax.numpy as jnp
from jax import lax
from jax.sharding import PartitionSpec as P


def combined_all(value, axis, join):
    pieces = jax.tree.map(lambda part: lax.all_gather(part, axis), value)
    head = jax.tree.map(lambda part: part[0], pieces)
    tail = jax.tree.map(lambda part: part[1:], pieces)
    total, _ = lax.scan(lambda total, slab: (join(total, slab), None), head, tail)
    return total


def combine_lse(first, second):
    peak = jnp.maximum(first[0], second[0])
    total = first[1] * jnp.exp(first[0] - peak) + second[1] * jnp.exp(second[0] - peak)
    return (peak, total)


def shards(image_emb, text_emb, logit_scale):
    row_count = lax.axis_size("row")
    col_count = lax.axis_size("col")
    row_index = lax.axis_index("row")
    col_index = lax.axis_index("col")
    pairs_each = image_emb.shape[0]
    width = image_emb.shape[2]
    block_rows = pairs_each * col_count
    block_cols = pairs_each * row_count
    total_pairs = block_rows * row_count
    factor = logit_scale[0]
    images = lax.all_gather(image_emb, "col", axis=1, tiled=True).reshape(block_rows, width)
    texts = lax.all_gather(text_emb, "row", axis=1, tiled=True).reshape(block_cols, width)
    scores = factor * lax.dot_general(
        images, texts, (((1,), (1,)), ((), ())), preferred_element_type=jnp.float32
    )
    row_ids = row_index * block_rows + jnp.arange(block_rows, dtype=jnp.int32)
    col_ids = col_index * block_cols + jnp.arange(block_cols, dtype=jnp.int32)
    eye = row_ids[:, None] == col_ids[None, :]
    local_row_peak = jnp.max(scores, axis=1)
    local_col_peak = jnp.max(scores, axis=0)
    row_local = jnp.sum(jnp.exp(scores - local_row_peak[:, None]), axis=1)
    col_local = jnp.sum(jnp.exp(scores - local_col_peak[None, :]), axis=0)
    row_peak, row_total = combined_all((local_row_peak, row_local), "col", combine_lse)
    col_peak, col_total = combined_all((local_col_peak, col_local), "row", combine_lse)
    row_lse = row_peak + jnp.log(row_total)
    col_lse = col_peak + jnp.log(col_total)
    local_loss = jnp.where(col_index == 0, jnp.sum(row_lse), 0.0) + jnp.where(
        row_index == 0, jnp.sum(col_lse), 0.0
    )
    local_loss = local_loss - 2.0 * jnp.sum(jnp.where(eye, scores, 0.0))
    loss = lax.psum(local_loss, ("row", "col")) / (2.0 * total_pairs)
    delta = factor * (
        jnp.exp(scores - row_lse[:, None])
        + jnp.exp(scores - col_lse[None, :])
        - 2.0 * eye.astype(jnp.float32)
    )
    delta = delta.astype(jnp.bfloat16)
    image_part = jnp.dot(delta, texts, preferred_element_type=jnp.float32).reshape(
        pairs_each, col_count, width
    )
    text_part = lax.dot_general(
        delta, images, (((0,), (0,)), ((), ())), preferred_element_type=jnp.float32
    )
    text_part = text_part.reshape(pairs_each, row_count, width)
    image_grad = lax.psum_scatter(image_part, "col", scatter_dimension=1, tiled=True)
    text_grad = lax.psum_scatter(text_part, "row", scatter_dimension=1, tiled=True)
    return (loss, image_grad, text_grad)


def solution(mesh):
    placed = (P("row", "col", None), P("col", "row", None), P())
    return jax.shard_map(
        shards,
        mesh=mesh,
        in_specs=placed,
        out_specs=(P(), P("row", "col", None), P("col", "row", None)),
        check_vma=False,
    )
```

profile of v0, /device:TPU:0, one launch (start us, length us, event | category | flops | bytes accessed | tf_op | source)
XLA Modules:
  0.0 192.2 jit_solution(12539619341615813686)
XLA Ops:
  7.2 0.0 reduce-scatter.3.cloned.1.call-start
  7.9 6.7 %all_gather.30 = bf16[16,4,1024]{2,0,1:T(8,128)(2,1)S(1)} all-gather(bf16[16,1,1024]{2,0,1:T(8,128)(2,1)} %param.7), channel_id=1, replica_groups=mesh['row'=8,'col'=4] {'col'}, dimensions={1}, use_global_device_ids=true | all-gather | bytes 163840 | tf_op jit(solution)/shard_map/all_gather | solution.py:32
  14.6 0.1 copy.16
  14.7 0.0 copy-start
  14.8 0.7 copy-done
  15.5 0.0 copy-start.3
  15.5 31.7 %all_gather.31 = bf16[16,8,1024]{2,0,1:T(8,128)(2,1)S(1)} all-gather(bf16[16,1,1024]{2,0,1:T(8,128)(2,1)S(1)} %copy-done), channel_id=1, replica_groups=mesh['row'=8,'col'=4] {'row'}, dimensions={1}, use_global_device_ids=true | all-gather | bytes 294912 | tf_op jit(solution)/shard_map/all_gather | solution.py:33
  47.1 0.0 copy-done.3
  47.1 0.6 dynamic-slice
  48.4 0.4 fusion.24
  48.8 0.2 dynamic-update-slice
  49.0 0.7 fusion.15
  49.7 0.2 dynamic-update-slice.1
  49.9 5.6 %all-reduce.2 = (f32[256]{0:T(256)S(1)}, f32[256]{0:T(256)S(1)}) all-reduce(f32[256]{0:T(256)S(1)} %dynamic-update-slice, f32[256]{0:T(256)S(1)} %dynamic-update-slice.1), channel_id=2, replica_groups=mesh['row'=8,'col'=4] {'col'}, use_global_device_ids=true, to_apply=%add | all-reduce | flops 512 | bytes 4096
  55.6 0.1 slice.34
  55.6 0.1 slice.35
  55.7 20.2 %all-gather.5 = f32[8,1,128]{2,1,0:T(1,128)S(1)} all-gather(f32[1,1,128]{2,1,0:T(1,128)S(1)} %bitcast.71), channel_id=5, replica_groups=mesh['row'=8,'col'=4] {'row'}, dimensions={0}, use_global_device_ids=true | all-gather | bytes 4608 | tf_op jit(solution)/shard_map/all_gather | solution.py:8
  75.9 0.0 copy-start.1
  75.9 0.6 copy-done.1
  76.5 16.1 %all-gather.4 = f32[8,1,128]{2,1,0:T(1,128)S(1)} all-gather(f32[1,1,128]{2,1,0:T(1,128)S(1)} %bitcast.70), channel_id=4, replica_groups=mesh['row'=8,'col'=4] {'row'}, dimensions={0}, use_global_device_ids=true | all-gather | bytes 4608 | tf_op jit(solution)/shard_map/all_gather | solution.py:8
  92.7 0.0 copy-start.2
  92.7 0.6 copy-done.2
  93.3 0.1 reshape.39
  93.3 0.1 reshape.38
  93.4 0.0 slice-start
  93.4 0.1 while.24
  93.5 0.6 slice-done
  94.1 0.0 slice-start.1
  94.1 0.7 slice-done.1
  94.8 0.3 while.25
  95.1 0.6 fusion.28
  95.7 0.6 fusion.27
  96.3 0.1 fusion.18
  96.4 1.0 fusion.10
  97.4 0.0 reduce-scatter.3.cloned.1.call-update
  97.4 0.0 reduce-scatter.5.cloned.1.call-start
  97.5 0.1 fusion.20
  97.6 0.1 copy.19
  97.7 1.0 fusion.21
  98.7 0.0 reduce-scatter.5.cloned.1.call-update
  100.6 38.6 %psum.7 = f32[]{:T(128)} all-reduce(f32[]{:T(128)S(6)} %sub.61), channel_id=1, replica_groups=mesh['row'=8,'col'=4] {'row','col'}, use_global_device_ids=true, to_apply=%region_11.12 | all-reduce | flops 1 | bytes 8 | tf_op jit(solution)/shard_map/psum | solution.py:52
  139.9 0.0 reduce-scatter.3.cloned.1.call-done
  139.9 1.5 copy.21
  141.5 41.2 %reduce-scatter.5.cloned.1.call-done = f32[16,1,1024]{2,0,1:T(8,128)} async-done(((f32[16,8,1024]{2,0,1:T(8,128)}), f32[16,1,1024]{2,0,1:T(8,128)}) %reduce-scatter.5.cloned.1.call-update) | async-done | bytes 65552 | tf_op jit(solution)/shard_map/reduce_scatter | solution.py:67
  182.7 1.5 copy.22
  (22 shorter events, 0.4 us)
Async XLA Ops:
  7.2 132.7 %reduce-scatter.3.cloned.1.call-start = ((), (), s32[]{:S(2)}) async-start(), calls=%async_computation.2 | async-start | bytes 327680 | tf_op jit(solution)/shard_map/reduce_scatter | solution.py:66
  14.7 0.8 copy-start
  15.5 31.7 %copy-start.3 = (u32[32]{0:T(128)S(1)}, u32[32]{0:T(128)}, u32[]{:S(2)}) copy-start(u32[32]{0:T(128)} %constant.46) | copy-start | bytes 388
  75.9 0.6 copy-start.1
  92.7 0.6 copy-start.2
  93.4 0.7 slice-start
  94.1 0.7 slice-start.1
  97.4 85.3 %reduce-scatter.5.cloned.1.call-start = ((), (), s32[]{:S(2)}) async-start(), calls=%async_computation.3 | async-start | bytes 589824 | tf_op jit(solution)/shard_map/reduce_scatter | solution.py:67
Sparse Core Ops, SparseCore 0:
  97.5 19.0 reduce-scatter.2
  120.3 62.3 reduce-scatter.4
where the time goes:
time: 193 us; the launch traced here: 192 us
  blocking collectives  119 us (62%)
  waiting for transfers between devices  41.3 us (21%)
  between operations  19.1 us (10%)
  local copies, waits for them, and re-layouts  7.86 us (4%)
  matrix products  2.39 us (1%)
  other arithmetic  2.36 us (1%)
    reduce_scatter x1, waiting for transfers between devices, shards(): lax.psum_scatter(text_part, 'row', scatter_dimension=1, tiled=True)  41.2 us
    psum x1, blocking collectives, shards(): loss = lax.psum(local_loss, ('row', 'col')) / (2.0 * total_pairs)  38.6 us
    all_gather x2, blocking collectives, combined_all(): pieces = jax.tree.map(lambda part: lax.all_gather(part, axis), value)  36.4 us
    all_gather x1, blocking collectives, shards(): lax.all_gather(text_emb, 'row', axis=1, tiled=True)  31.7 us
    all_gather x1, blocking collectives, shards(): lax.all_gather(image_emb, 'col', axis=1, tiled=True)  6.72 us
    unnamed x17, local copies, waits for them, and re-layouts  5.99 us
    unnamed x1, blocking collectives  5.63 us
  transfers between devices with their start and end apart: 2, of which 1 were waited for; matrix products, arithmetic and copies ran while one was open for 1% of the time, Pallas kernels for 0%

commit v1 on v0

v1 whole, which is shorter than its diff:
```python
import functools

import jax
import jax.numpy as jnp
from jax import lax
from jax.experimental import pallas as pl
from jax.experimental.pallas import tpu as pltpu
from jax.sharding import PartitionSpec as P

MESH = pl.DeviceIdType.MESH
F32 = jnp.float32


def kernel(
    nr, nc, img_hbm, txt_hbm, scale,
    loss_ref, ig_ref, tg_ref,
    imgs, txts, rstat, cstat, iout, tout, iin, tin, iown, town, lrow, lcol,
    local_sem, send_sem, recv_sem,
):
    r = lax.axis_index("row")
    c = lax.axis_index("col")
    m, width = img_hbm.shape
    br, bc = m * nc, m * nr
    rows = [lax.rem(r + d, nr) for d in range(1, nr)]
    cols = [lax.rem(c + d, nc) for d in range(1, nc)]

    li = pltpu.make_async_copy(img_hbm, imgs.at[c], local_sem.at[0])
    lt = pltpu.make_async_copy(txt_hbm, txts.at[r], local_sem.at[1])
    li.start()
    lt.start()
    barrier = pltpu.get_barrier_semaphore()
    for p in rows:
        pl.semaphore_signal(barrier, inc=1, device_id=(p, c), device_id_type=MESH)
    for p in cols:
        pl.semaphore_signal(barrier, inc=1, device_id=(r, p), device_id_type=MESH)
    lt.wait()
    li.wait()
    pl.semaphore_wait(barrier, nr + nc - 2)

    def push(src, dst, k, dev):
        pltpu.make_async_remote_copy(
            src_ref=src, dst_ref=dst, send_sem=send_sem.at[k], recv_sem=recv_sem.at[k],
            device_id=dev, device_id_type=MESH,
        ).start()

    def arrived(ref, n, k):
        part = ref.at[pl.ds(0, n)]
        pltpu.make_async_copy(part, part, recv_sem.at[k]).wait()

    def left(ref, n, k):
        part = ref.at[pl.ds(0, n)]
        pltpu.make_async_copy(part, part, send_sem.at[k]).wait()

    for p in rows:
        push(txts.at[r], txts.at[r], 0, (p, c))
    for p in cols:
        push(imgs.at[c], imgs.at[c], 1, (r, p))
    factor = scale[0]
    arrived(imgs, nc - 1, 1)
    images = imgs[...].reshape(br, width)
    arrived(txts, nr - 1, 0)
    texts = txts[...].reshape(bc, width)
    s = factor * lax.dot_general(images, texts, (((1,), (1,)), ((), ())), preferred_element_type=F32)
    st = s.T

    def pair_i(i):
        return (r * m + lax.rem(i, m)) * nc + lax.div(i, m)

    def pair_t(i):
        return (c * m + lax.rem(i, m)) * nr + lax.div(i, m)

    eye = pair_i(lax.broadcasted_iota(jnp.int32, (br, bc), 0)) == pair_t(
        lax.broadcasted_iota(jnp.int32, (br, bc), 1)
    )
    eye_t = pair_t(lax.broadcasted_iota(jnp.int32, (bc, br), 0)) == pair_i(
        lax.broadcasted_iota(jnp.int32, (bc, br), 1)
    )

    cpeak = jnp.max(s, axis=0, keepdims=True)
    csum = jnp.sum(jnp.exp(s - cpeak), axis=0, keepdims=True)
    which = lax.broadcasted_iota(jnp.int32, (8, bc), 0)
    cstat[r] = jnp.where(which == 0, cpeak, csum)
    for p in rows:
        push(cstat.at[r], cstat.at[r], 2, (p, c))
    rpeak = jnp.max(st, axis=0, keepdims=True)
    rsum = jnp.sum(jnp.exp(st - rpeak), axis=0, keepdims=True)
    rdiag = jnp.sum(jnp.where(eye_t, st, 0.0), axis=0, keepdims=True)
    which = lax.broadcasted_iota(jnp.int32, (8, br), 0)
    rstat[c] = jnp.where(which == 0, rpeak, jnp.where(which == 1, rsum, rdiag))
    for p in cols:
        push(rstat.at[c], rstat.at[c], 3, (r, p))

    def lse(ref, n):
        peak = ref[0, 0:1, :]
        for k in range(1, n):
            peak = jnp.maximum(peak, ref[k, 0:1, :])
        total = jnp.zeros_like(peak)
        for k in range(n):
            total = total + ref[k, 1:2, :] * jnp.exp(ref[k, 0:1, :] - peak)
        return peak + jnp.log(total)

    arrived(rstat, nc - 1, 3)
    row_lse = lse(rstat, nc)
    diag = rstat[0, 2:3, :]
    for k in range(1, nc):
        diag = diag + rstat[k, 2:3, :]
    row_term = jnp.exp(s - jnp.broadcast_to(row_lse, (bc, br)).T) - jnp.where(eye, 2.0, 0.0)
    arrived(cstat, nr - 1, 2)
    col_lse = lse(cstat, nr)
    delta = factor * (row_term + jnp.exp(s - col_lse))
    delta_t = delta.T.astype(jnp.bfloat16)
    delta = delta.astype(jnp.bfloat16)

    tpart = jnp.dot(delta_t, images, preferred_element_type=F32).reshape(nr, m, width)
    town[...] = tpart
    tout[...] = tpart.astype(jnp.bfloat16)
    for d, p in enumerate(rows):
        push(tout.at[p], tin.at[d], 4, (p, c))
    ipart = jnp.dot(delta, texts, preferred_element_type=F32).reshape(nc, m, width)
    iown[...] = ipart
    iout[...] = ipart.astype(jnp.bfloat16)
    for d, p in enumerate(cols):
        push(iout.at[p], iin.at[d], 5, (r, p))

    lrow[r] = jnp.broadcast_to(jnp.sum(row_lse - 2.0 * diag, axis=1, keepdims=True), (8, 128))
    lcol[c] = jnp.broadcast_to(jnp.sum(col_lse, axis=1, keepdims=True), (8, 128))
    for p in rows:
        push(lrow.at[r], lrow.at[r], 6, (p, c))
    for p in cols:
        push(lcol.at[c], lcol.at[c], 7, (r, p))

    arrived(iin, nc - 1, 5)
    total = iown[c]
    for d in range(nc - 1):
        total = total + iin[d].astype(F32)
    ig_ref[...] = total
    arrived(tin, nr - 1, 4)
    total = town[r]
    for d in range(nr - 1):
        total = total + tin[d].astype(F32)
    tg_ref[...] = total
    arrived(lrow, nr - 1, 6)
    arrived(lcol, nc - 1, 7)
    total = lrow[0]
    for k in range(1, nr):
        total = total + lrow[k]
    for k in range(nc):
        total = total + lcol[k]
    loss_ref[0] = total[0, 0] / (2.0 * br * nr)

    left(txts, nr - 1, 0)
    left(imgs, nc - 1, 1)
    left(cstat, nr - 1, 2)
    left(rstat, nc - 1, 3)
    left(tin, nr - 1, 4)
    left(iin, nc - 1, 5)
    left(lrow, nr - 1, 6)
    left(lcol, nc - 1, 7)


def shards(nr, nc, image_emb, text_emb, logit_scale):
    m, _, width = image_emb.shape
    br, bc = m * nc, m * nr
    bf16 = jnp.bfloat16
    loss, ig, tg = pl.pallas_call(
        functools.partial(kernel, nr, nc),
        out_shape=(
            jax.ShapeDtypeStruct((1,), F32),
            jax.ShapeDtypeStruct((m, width), F32),
            jax.ShapeDtypeStruct((m, width), F32),
        ),
        in_specs=[
            pl.BlockSpec(memory_space=pl.ANY),
            pl.BlockSpec(memory_space=pl.ANY),
            pl.BlockSpec(memory_space=pltpu.SMEM),
        ],
        out_specs=(
            pl.BlockSpec(memory_space=pltpu.SMEM),
            pl.BlockSpec(memory_space=pltpu.VMEM),
            pl.BlockSpec(memory_space=pltpu.VMEM),
        ),
        scratch_shapes=[
            pltpu.VMEM((nc, m, width), bf16),
            pltpu.VMEM((nr, m, width), bf16),
            pltpu.VMEM((nc, 8, br), F32),
            pltpu.VMEM((nr, 8, bc), F32),
            pltpu.VMEM((nc, m, width), bf16),
            pltpu.VMEM((nr, m, width), bf16),
            pltpu.VMEM((nc - 1, m, width), bf16),
            pltpu.VMEM((nr - 1, m, width), bf16),
            pltpu.VMEM((nc, m, width), F32),
            pltpu.VMEM((nr, m, width), F32),
            pltpu.VMEM((nr, 8, 128), F32),
            pltpu.VMEM((nc, 8, 128), F32),
            pltpu.SemaphoreType.DMA((2,)),
            pltpu.SemaphoreType.DMA((8,)),
            pltpu.SemaphoreType.DMA((8,)),
        ],
        compiler_params=pltpu.CompilerParams(
            collective_id=0, has_side_effects=True, vmem_limit_bytes=40 * 1024 * 1024
        ),
    )(image_emb.reshape(m, width), text_emb.reshape(m, width), logit_scale)
    return loss[0], ig.reshape(m, 1, width), tg.reshape(m, 1, width)


def solution(mesh):
    return jax.shard_map(
        functools.partial(shards, mesh.shape["row"], mesh.shape["col"]),
        mesh=mesh,
        in_specs=(P("row", "col", None), P("col", "row", None), P()),
        out_specs=(P(), P("row", "col", None), P("col", "row", None)),
        check_vma=False,
    )
```

time: 193 us -> 32.4 us (0.17)
  blocking collectives: 119 us -> 0 us
  waiting for transfers between devices: 41.3 us -> 0 us
  Pallas kernels: 0 us -> 26.2 us
  between operations: 19.1 us -> 3.06 us
  local copies, waits for them, and re-layouts: 7.86 us -> 2.9 us
  matrix products: 2.39 us -> 0 us
  other arithmetic: 2.36 us -> 0 us
    all_gather x4 -> x0, blocking collectives: 74.8 us -> none  [the longest x2 36.4 us: combined_all(): pieces = jax.tree.map(lambda part: lax.all_gather(part, axis), value)]
    reduce_scatter x2 -> x0, waiting for transfers between devices: 41.2 us -> none  [the longest x1 41.2 us: shards(): lax.psum_scatter(text_part, 'row', scatter_dimension=1, tiled=True)]
    psum x1 -> x0, blocking collectives: 38.6 us -> none  [shards(): loss = lax.psum(local_loss, ('row', 'col')) / (2.0 * total_pairs)]
    pallas_call x0 -> x1, Pallas kernels: none -> 26.2 us  [shards(): pl.pallas_call(functools.partial(kernel, nr, nc), out_shape=(jax.ShapeDty...]
    unnamed x1 -> x0, blocking collectives: 5.63 us -> none
    unnamed x17 -> x6, local copies, waits for them, and re-layouts: 5.99 us -> 2.9 us
    dot_general x3 -> x0, matrix products: 2.39 us -> none  [the longest x1 1.01 us: shards(): lax.dot_general(delta, images, (((0,), (0,)), ((), ())), preferred_elemen...]
  transfers between devices with their start and end apart: 2 -> 0, of which waited for: 1 -> 0; matrix products, arithmetic and copies ran while one was open for 1% -> 0% of each run, Pallas kernels for 0% -> 0%
where the time goes in v1:
time: 32.4 us; the launch traced here: 32.1 us
  Pallas kernels  26.2 us (81%)
  between operations  3.06 us (9%)
  local copies, waits for them, and re-layouts  2.9 us (9%)
    pallas_call x1, Pallas kernels, shards(): pl.pallas_call(functools.partial(kernel, nr, nc), out_shape=(jax.ShapeDty...  26.2 us
    unnamed x6, local copies, waits for them, and re-layouts  2.9 us

profile of v1, /device:TPU:0, one launch (start us, length us, event | category | flops | bytes accessed | tf_op | source)
XLA Modules:
  0.0 32.1 jit_solution(18371684183612321730)
XLA Ops:
  1.3 0.0 copy-start
  1.3 0.7 %copy-done = bf16[16,1,1024]{2,0,1:T(8,128)(2,1)S(1)} copy-done((bf16[16,1,1024]{2,0,1:T(8,128)(2,1)S(1)}, bf16[16,1,1024]{2,0,1:T(8,128)(2,1)}, u32[]{:S(2)}) %copy-start) | copy-done | bytes 32792
  2.0 0.0 copy-start.1
  2.0 0.8 %copy-done.1 = bf16[16,1,1024]{2,0,1:T(8,128)(2,1)S(1)} copy-done((bf16[16,1,1024]{2,0,1:T(8,128)(2,1)S(1)}, bf16[16,1,1024]{2,0,1:T(8,128)(2,1)}, u32[]{:S(2)}) %copy-start.1) | copy-done | bytes 32792
  2.8 26.2 %shard_map.58 = (f32[1]{0:T(128)}, f32[16,1024]{1,0:T(8,128)S(1)}, f32[16,1024]{1,0:T(8,128)S(1)}) custom-call(bf16[16,1024]{1,0:T(8,128)(2,1)S(1)} %bitcast.7, bf16[16,1024]{1,0:T(8,128)(2,1)S(1)} %bitcast.8, f32[1]{0:T(128)S(6)} %copy.9.scale), custom_call_target="tpu_custom_call" | custom-call | tf_op jit(solution)/shard_map/pallas_call | solution.py:165
  29.0 0.7 %copy.6 = f32[16,1,1024]{2,1,0:T(1,128)} copy(f32[16,1,1024]{2,0,1:T(8,128)S(1)} %bitcast.6) | data formatting | bytes 131072
  29.7 0.7 %copy.7 = f32[16,1,1024]{2,1,0:T(1,128)} copy(f32[16,1,1024]{2,0,1:T(8,128)S(1)} %bitcast.5) | data formatting | bytes 131072
Async XLA Ops:
  1.3 0.8 %copy-start = (bf16[16,1,1024]{2,0,1:T(8,128)(2,1)S(1)}, bf16[16,1,1024]{2,0,1:T(8,128)(2,1)}, u32[]{:S(2)}) copy-start(bf16[16,1,1024]{2,0,1:T(8,128)(2,1)} %param.3) | copy-start | bytes 98308
  2.0 0.8 %copy-start.1 = (bf16[16,1,1024]{2,0,1:T(8,128)(2,1)S(1)}, bf16[16,1,1024]{2,0,1:T(8,128)(2,1)}, u32[]{:S(2)}) copy-start(bf16[16,1,1024]{2,0,1:T(8,128)(2,1)} %param.4) | copy-start | bytes 98308

commit v2 on v1

v2 whole, which is shorter than its diff:
```python
import functools

import jax
import jax.numpy as jnp
from jax import lax
from jax.experimental import pallas as pl
from jax.experimental.pallas import tpu as pltpu
from jax.sharding import PartitionSpec as P

MESH = pl.DeviceIdType.MESH
F32 = jnp.float32


def kernel(
    nr, nc, lo, img_hbm, txt_hbm, scale,
    loss_ref, ig_ref, tg_ref,
    imgs, txts, rstat, cstat, iout, tout, iin, tin, iown, town, lrow, lcol,
    local_sem, send_sem, recv_sem,
):
    r = lax.axis_index("row")
    c = lax.axis_index("col")
    m, width = img_hbm.shape
    ni, nt = nr // lo, lo * nc
    br, bc = m * ni, m * nt
    hi_me, lo_me = lax.div(r, lo), lax.rem(r, lo)
    a, b = hi_me, lo_me * nc + c
    ipeers = [lax.rem(a + d, ni) for d in range(1, ni)]
    tpeers = [lax.rem(b + d, nt) for d in range(1, nt)]

    def idev(k):
        return (k * lo + lo_me, c)

    def tdev(q):
        return (hi_me * lo + lax.div(q, nc), lax.rem(q, nc))

    li = pltpu.make_async_copy(img_hbm, imgs.at[a], local_sem.at[0])
    lt = pltpu.make_async_copy(txt_hbm, txts.at[b], local_sem.at[1])
    li.start()
    lt.start()
    barrier = pltpu.get_barrier_semaphore()
    for p in tpeers:
        pl.semaphore_signal(barrier, inc=1, device_id=tdev(p), device_id_type=MESH)
    for p in ipeers:
        pl.semaphore_signal(barrier, inc=1, device_id=idev(p), device_id_type=MESH)
    lt.wait()
    li.wait()
    pl.semaphore_wait(barrier, ni + nt - 2)

    def push(src, dst, k, dev):
        pltpu.make_async_remote_copy(
            src_ref=src, dst_ref=dst, send_sem=send_sem.at[k], recv_sem=recv_sem.at[k],
            device_id=dev, device_id_type=MESH,
        ).start()

    def arrived(ref, n, k):
        part = ref.at[pl.ds(0, n)]
        pltpu.make_async_copy(part, part, recv_sem.at[k]).wait()

    def left(ref, n, k):
        part = ref.at[pl.ds(0, n)]
        pltpu.make_async_copy(part, part, send_sem.at[k]).wait()

    for p in tpeers:
        push(txts.at[b], txts.at[b], 0, tdev(p))
    for p in ipeers:
        push(imgs.at[a], imgs.at[a], 1, idev(p))
    factor = scale[0]
    arrived(imgs, ni - 1, 1)
    images = imgs[...].reshape(br, width)
    arrived(txts, nt - 1, 0)
    texts = txts[...].reshape(bc, width)
    s = factor * lax.dot_general(images, texts, (((1,), (1,)), ((), ())), preferred_element_type=F32)
    st = s.T

    def pair_i(i):
        return ((lax.div(i, m) * lo + lo_me) * m + lax.rem(i, m)) * nc + c

    def pair_t(i):
        q = lax.div(i, m)
        return (lax.rem(q, nc) * m + lax.rem(i, m)) * nr + hi_me * lo + lax.div(q, nc)

    eye = pair_i(lax.broadcasted_iota(jnp.int32, (br, bc), 0)) == pair_t(
        lax.broadcasted_iota(jnp.int32, (br, bc), 1)
    )
    eye_t = pair_t(lax.broadcasted_iota(jnp.int32, (bc, br), 0)) == pair_i(
        lax.broadcasted_iota(jnp.int32, (bc, br), 1)
    )

    cpeak = jnp.max(s, axis=0, keepdims=True)
    csum = jnp.sum(jnp.exp(s - cpeak), axis=0, keepdims=True)
    which = lax.broadcasted_iota(jnp.int32, (8, bc), 0)
    cstat[b] = jnp.where(which == 0, cpeak, csum)
    for p in tpeers:
        push(cstat.at[b], cstat.at[b], 2, tdev(p))
    rpeak = jnp.max(st, axis=0, keepdims=True)
    rsum = jnp.sum(jnp.exp(st - rpeak), axis=0, keepdims=True)
    rdiag = jnp.sum(jnp.where(eye_t, st, 0.0), axis=0, keepdims=True)
    which = lax.broadcasted_iota(jnp.int32, (8, br), 0)
    rstat[a] = jnp.where(which == 0, rpeak, jnp.where(which == 1, rsum, rdiag))
    for p in ipeers:
        push(rstat.at[a], rstat.at[a], 3, idev(p))

    def lse(ref, n):
        peak = ref[0, 0:1, :]
        for k in range(1, n):
            peak = jnp.maximum(peak, ref[k, 0:1, :])
        total = jnp.zeros_like(peak)
        for k in range(n):
            total = total + ref[k, 1:2, :] * jnp.exp(ref[k, 0:1, :] - peak)
        return peak + jnp.log(total)

    arrived(rstat, ni - 1, 3)
    row_lse = lse(rstat, ni)
    diag = rstat[0, 2:3, :]
    for k in range(1, ni):
        diag = diag + rstat[k, 2:3, :]
    row_term = jnp.exp(s - jnp.broadcast_to(row_lse, (bc, br)).T) - jnp.where(eye, 2.0, 0.0)
    arrived(cstat, nt - 1, 2)
    col_lse = lse(cstat, nt)
    delta = factor * (row_term + jnp.exp(s - col_lse))
    delta_t = delta.T.astype(jnp.bfloat16)
    delta = delta.astype(jnp.bfloat16)

    tpart = jnp.dot(delta_t, images, preferred_element_type=F32).reshape(nt, m, width)
    town[...] = tpart
    tout[...] = tpart.astype(jnp.bfloat16)
    for d, p in enumerate(tpeers):
        push(tout.at[p], tin.at[d], 4, tdev(p))
    ipart = jnp.dot(delta, texts, preferred_element_type=F32).reshape(ni, m, width)
    iown[...] = ipart
    iout[...] = ipart.astype(jnp.bfloat16)
    for d, p in enumerate(ipeers):
        push(iout.at[p], iin.at[d], 5, idev(p))

    lrow[b] = jnp.broadcast_to(jnp.sum(row_lse - 2.0 * diag, axis=1, keepdims=True), (8, 128))
    lcol[a] = jnp.broadcast_to(jnp.sum(col_lse, axis=1, keepdims=True), (8, 128))
    for p in tpeers:
        push(lrow.at[b], lrow.at[b], 6, tdev(p))
    for p in ipeers:
        push(lcol.at[a], lcol.at[a], 7, idev(p))

    arrived(iin, ni - 1, 5)
    total = iown[a]
    for d in range(ni - 1):
        total = total + iin[d].astype(F32)
    ig_ref[...] = total
    arrived(tin, nt - 1, 4)
    total = town[b]
    for d in range(nt - 1):
        total = total + tin[d].astype(F32)
    tg_ref[...] = total
    arrived(lrow, nt - 1, 6)
    arrived(lcol, ni - 1, 7)
    total = lrow[0]
    for k in range(1, nt):
        total = total + lrow[k]
    for k in range(ni):
        total = total + lcol[k]
    loss_ref[0] = total[0, 0] / (2.0 * m * nr * nc)

    left(txts, nt - 1, 0)
    left(imgs, ni - 1, 1)
    left(cstat, nt - 1, 2)
    left(rstat, ni - 1, 3)
    left(tin, nt - 1, 4)
    left(iin, ni - 1, 5)
    left(lrow, nt - 1, 6)
    left(lcol, ni - 1, 7)


def shards(nr, nc, image_emb, text_emb, logit_scale):
    m, _, width = image_emb.shape
    lo = 2 if nr % 2 == 0 else 1
    ni, nt = nr // lo, lo * nc
    br, bc = m * ni, m * nt
    bf16 = jnp.bfloat16
    loss, ig, tg = pl.pallas_call(
        functools.partial(kernel, nr, nc, lo),
        out_shape=(
            jax.ShapeDtypeStruct((1,), F32),
            jax.ShapeDtypeStruct((m, width), F32),
            jax.ShapeDtypeStruct((m, width), F32),
        ),
        in_specs=[
            pl.BlockSpec(memory_space=pltpu.HBM),
            pl.BlockSpec(memory_space=pltpu.HBM),
            pl.BlockSpec(memory_space=pltpu.SMEM),
        ],
        out_specs=(
            pl.BlockSpec(memory_space=pltpu.SMEM),
            pl.BlockSpec(memory_space=pltpu.VMEM),
            pl.BlockSpec(memory_space=pltpu.VMEM),
        ),
        scratch_shapes=[
            pltpu.VMEM((ni, m, width), bf16),
            pltpu.VMEM((nt, m, width), bf16),
            pltpu.VMEM((ni, 8, br), F32),
            pltpu.VMEM((nt, 8, bc), F32),
            pltpu.VMEM((ni, m, width), bf16),
            pltpu.VMEM((nt, m, width), bf16),
            pltpu.VMEM((ni - 1, m, width), bf16),
            pltpu.VMEM((nt - 1, m, width), bf16),
            pltpu.VMEM((ni, m, width), F32),
            pltpu.VMEM((nt, m, width), F32),
            pltpu.VMEM((nt, 8, 128), F32),
            pltpu.VMEM((ni, 8, 128), F32),
            pltpu.SemaphoreType.DMA((2,)),
            pltpu.SemaphoreType.DMA((8,)),
            pltpu.SemaphoreType.DMA((8,)),
        ],
        compiler_params=pltpu.CompilerParams(
            collective_id=0, has_side_effects=True, vmem_limit_bytes=40 * 1024 * 1024
        ),
    )(image_emb.reshape(m, width), text_emb.reshape(m, width), logit_scale)
    return loss[0], ig.reshape(m, 1, width), tg.reshape(m, 1, width)


def solution(mesh):
    return jax.shard_map(
        functools.partial(shards, mesh.shape["row"], mesh.shape["col"]),
        mesh=mesh,
        in_specs=(P("row", "col", None), P("col", "row", None), P()),
        out_specs=(P(), P("row", "col", None), P("col", "row", None)),
        check_vma=False,
    )
```

time: 32.4 us -> 26.8 us (0.83)
  Pallas kernels: 26.2 us -> 20.5 us
    pallas_call x1, Pallas kernels: 26.2 us -> 20.5 us  [shards(): pl.pallas_call(functools.partial(kernel, nr, nc, lo), out_shape=(jax.Shap...]
where the time goes in v2:
time: 26.8 us; the launch traced here: 26.5 us
  Pallas kernels  20.5 us (76%)
  between operations  3.06 us (11%)
  local copies, waits for them, and re-layouts  2.9 us (11%)
    pallas_call x1, Pallas kernels, shards(): pl.pallas_call(functools.partial(kernel, nr, nc, lo), out_shape=(jax.Shap...  20.5 us
    unnamed x6, local copies, waits for them, and re-layouts  2.9 us

profile of v2, /device:TPU:0, one launch (start us, length us, event | category | flops | bytes accessed | tf_op | source)
XLA Modules:
  0.0 26.5 jit_solution(14526822153054295931)
XLA Ops:
  1.3 0.0 copy-start
  1.3 0.7 %copy-done = bf16[16,1,1024]{2,0,1:T(8,128)(2,1)S(1)} copy-done((bf16[16,1,1024]{2,0,1:T(8,128)(2,1)S(1)}, bf16[16,1,1024]{2,0,1:T(8,128)(2,1)}, u32[]{:S(2)}) %copy-start) | copy-done | bytes 32792
  2.0 0.0 copy-start.1
  2.0 0.8 %copy-done.1 = bf16[16,1,1024]{2,0,1:T(8,128)(2,1)S(1)} copy-done((bf16[16,1,1024]{2,0,1:T(8,128)(2,1)S(1)}, bf16[16,1,1024]{2,0,1:T(8,128)(2,1)}, u32[]{:S(2)}) %copy-start.1) | copy-done | bytes 32792
  2.8 20.5 %shard_map.58 = (f32[1]{0:T(128)}, f32[16,1024]{1,0:T(8,128)S(1)}, f32[16,1024]{1,0:T(8,128)S(1)}) custom-call(bf16[16,1024]{1,0:T(8,128)(2,1)S(1)} %bitcast.7, bf16[16,1024]{1,0:T(8,128)(2,1)S(1)} %bitcast.8, f32[1]{0:T(128)S(6)} %copy.9.scale), custom_call_target="tpu_custom_call" | custom-call | tf_op jit(solution)/shard_map/pallas_call | solution.py:177
  23.3 0.7 %copy.6 = f32[16,1,1024]{2,1,0:T(1,128)} copy(f32[16,1,1024]{2,0,1:T(8,128)S(1)} %bitcast.6) | data formatting | bytes 131072
  24.0 0.7 %copy.7 = f32[16,1,1024]{2,1,0:T(1,128)} copy(f32[16,1,1024]{2,0,1:T(8,128)S(1)} %bitcast.5) | data formatting | bytes 131072
Async XLA Ops:
  1.3 0.8 %copy-start = (bf16[16,1,1024]{2,0,1:T(8,128)(2,1)S(1)}, bf16[16,1,1024]{2,0,1:T(8,128)(2,1)}, u32[]{:S(2)}) copy-start(bf16[16,1,1024]{2,0,1:T(8,128)(2,1)} %param.3) | copy-start | bytes 98308
  2.0 0.8 %copy-start.1 = (bf16[16,1,1024]{2,0,1:T(8,128)(2,1)S(1)}, bf16[16,1,1024]{2,0,1:T(8,128)(2,1)}, u32[]{:S(2)}) copy-start(bf16[16,1,1024]{2,0,1:T(8,128)(2,1)} %param.4) | copy-start | bytes 98308

commit v3 on v2

--- a/solution.py
+++ b/solution.py
@@ -14,7 +14,7 @@
 def kernel(
     nr, nc, lo, img_hbm, txt_hbm, scale,
     loss_ref, ig_ref, tg_ref,
-    imgs, txts, rstat, cstat, iout, tout, iin, tin, iown, town, lrow, lcol,
+    imgs, txts, rstat, cstat, iout, tout, iin, tin, idelta, tdelta, lrow, lcol,
     local_sem, send_sem, recv_sem,
 ):
     r = lax.axis_index("row")
@@ -42,8 +42,6 @@
         pl.semaphore_signal(barrier, inc=1, device_id=tdev(p), device_id_type=MESH)
     for p in ipeers:
         pl.semaphore_signal(barrier, inc=1, device_id=idev(p), device_id_type=MESH)
-    lt.wait()
-    li.wait()
     pl.semaphore_wait(barrier, ni + nt - 2)
 
     def push(src, dst, k, dev):
@@ -61,10 +59,12 @@
         pltpu.make_async_copy(part, part, send_sem.at[k]).wait()
 
     for p in tpeers:
-        push(txts.at[b], txts.at[b], 0, tdev(p))
-    for p in ipeers:
-        push(imgs.at[a], imgs.at[a], 1, idev(p))
+        push(txt_hbm, txts.at[b], 0, tdev(p))
+    for p in ipeers:
+        push(img_hbm, imgs.at[a], 1, idev(p))
     factor = scale[0]
+    li.wait()
+    lt.wait()
     arrived(imgs, ni - 1, 1)
     images = imgs[...].reshape(br, width)
     arrived(txts, nt - 1, 0)
@@ -79,21 +79,20 @@
         q = lax.div(i, m)
         return (lax.rem(q, nc) * m + lax.rem(i, m)) * nr + hi_me * lo + lax.div(q, nc)
 
-    eye = pair_i(lax.broadcasted_iota(jnp.int32, (br, bc), 0)) == pair_t(
-        lax.broadcasted_iota(jnp.int32, (br, bc), 1)
-    )
     eye_t = pair_t(lax.broadcasted_iota(jnp.int32, (bc, br), 0)) == pair_i(
         lax.broadcasted_iota(jnp.int32, (bc, br), 1)
     )
 
     cpeak = jnp.max(s, axis=0, keepdims=True)
-    csum = jnp.sum(jnp.exp(s - cpeak), axis=0, keepdims=True)
+    cexp = jnp.exp(s - cpeak)
+    csum = jnp.sum(cexp, axis=0, keepdims=True)
     which = lax.broadcasted_iota(jnp.int32, (8, bc), 0)
     cstat[b] = jnp.where(which == 0, cpeak, csum)
     for p in tpeers:
         push(cstat.at[b], cstat.at[b], 2, tdev(p))
     rpeak = jnp.max(st, axis=0, keepdims=True)
-    rsum = jnp.sum(jnp.exp(st - rpeak), axis=0, keepdims=True)
+    rexp = jnp.exp(st - rpeak)
+    rsum = jnp.sum(rexp, axis=0, keepdims=True)
     rdiag = jnp.sum(jnp.where(eye_t, st, 0.0), axis=0, keepdims=True)
     which = lax.broadcasted_iota(jnp.int32, (8, br), 0)
     rstat[a] = jnp.where(which == 0, rpeak, jnp.where(which == 1, rsum, rdiag))
@@ -114,24 +113,24 @@
     diag = rstat[0, 2:3, :]
     for k in range(1, ni):
         diag = diag + rstat[k, 2:3, :]
-    row_term = jnp.exp(s - jnp.broadcast_to(row_lse, (bc, br)).T) - jnp.where(eye, 2.0, 0.0)
+    row_term = factor * (rexp * jnp.exp(rpeak - row_lse) - jnp.where(eye_t, 2.0, 0.0))
     arrived(cstat, nt - 1, 2)
     col_lse = lse(cstat, nt)
-    delta = factor * (row_term + jnp.exp(s - col_lse))
-    delta_t = delta.T.astype(jnp.bfloat16)
-    delta = delta.astype(jnp.bfloat16)
-
-    tpart = jnp.dot(delta_t, images, preferred_element_type=F32).reshape(nt, m, width)
-    town[...] = tpart
-    tout[...] = tpart.astype(jnp.bfloat16)
+    col_term = factor * (cexp * jnp.exp(cpeak - col_lse))
+    delta = (row_term.T + col_term).astype(jnp.bfloat16)
+    delta_t = (row_term + col_term.T).astype(jnp.bfloat16)
+
+    ipart = jnp.dot(delta, texts, preferred_element_type=F32)
+    iout[...] = ipart.astype(jnp.bfloat16).reshape(ni, m, width)
+    for d, p in enumerate(ipeers):
+        push(iout.at[p], iin.at[d], 5, idev(p))
+    tpart = jnp.dot(delta_t, images, preferred_element_type=F32)
+    tout[...] = tpart.astype(jnp.bfloat16).reshape(nt, m, width)
     for d, p in enumerate(tpeers):
         push(tout.at[p], tin.at[d], 4, tdev(p))
-    ipart = jnp.dot(delta, texts, preferred_element_type=F32).reshape(ni, m, width)
-    iown[...] = ipart
-    iout[...] = ipart.astype(jnp.bfloat16)
-    for d, p in enumerate(ipeers):
-        push(iout.at[p], iin.at[d], 5, idev(p))
-
+
+    idelta[...] = delta.reshape(ni, m, bc)
+    tdelta[...] = delta_t.reshape(nt, m, br)
     lrow[b] = jnp.broadcast_to(jnp.sum(row_lse - 2.0 * diag, axis=1, keepdims=True), (8, 128))
     lcol[a] = jnp.broadcast_to(jnp.sum(col_lse, axis=1, keepdims=True), (8, 128))
     for p in tpeers:
@@ -139,16 +138,16 @@
     for p in ipeers:
         push(lcol.at[a], lcol.at[a], 7, idev(p))
 
+    image_total = jnp.dot(idelta[a], texts, preferred_element_type=F32)
+    text_total = jnp.dot(tdelta[b], images, preferred_element_type=F32)
     arrived(iin, ni - 1, 5)
-    total = iown[a]
     for d in range(ni - 1):
-        total = total + iin[d].astype(F32)
-    ig_ref[...] = total
+        image_total = image_total + iin[d].astype(F32)
+    ig_ref[...] = image_total
     arrived(tin, nt - 1, 4)
-    total = town[b]
     for d in range(nt - 1):
-        total = total + tin[d].astype(F32)
-    tg_ref[...] = total
+        text_total = text_total + tin[d].astype(F32)
+    tg_ref[...] = text_total
     arrived(lrow, nt - 1, 6)
     arrived(lcol, ni - 1, 7)
     total = lrow[0]
@@ -200,8 +199,8 @@
             pltpu.VMEM((nt, m, width), bf16),
             pltpu.VMEM((ni - 1, m, width), bf16),
             pltpu.VMEM((nt - 1, m, width), bf16),
-            pltpu.VMEM((ni, m, width), F32),
-            pltpu.VMEM((nt, m, width), F32),
+            pltpu.VMEM((ni, m, bc), bf16),
+            pltpu.VMEM((nt, m, br), bf16),
             pltpu.VMEM((nt, 8, 128), F32),
             pltpu.VMEM((ni, 8, 128), F32),
             pltpu.SemaphoreType.DMA((2,)),
@@ -211,7 +210,11 @@
         compiler_params=pltpu.CompilerParams(
             collective_id=0, has_side_effects=True, vmem_limit_bytes=40 * 1024 * 1024
         ),
-    )(image_emb.reshape(m, width), text_emb.reshape(m, width), logit_scale)
+    )(
+        pltpu.with_memory_space_constraint(image_emb.reshape(m, width), pltpu.HBM),
+        pltpu.with_memory_space_constraint(text_emb.reshape(m, width), pltpu.HBM),
+        logit_scale,
+    )
     return loss[0], ig.reshape(m, 1, width), tg.reshape(m, 1, width)
 
 

time: 26.8 us -> 25.2 us (0.940)
  local copies, waits for them, and re-layouts: 2.9 us -> 1.39 us
    unnamed x6 -> x2, local copies, waits for them, and re-layouts: 2.9 us -> 1.39 us
where the time goes in v3:
time: 25.2 us; the launch traced here: 25 us
  Pallas kernels  20.7 us (82%)
  between operations  2.97 us (12%)
  local copies, waits for them, and re-layouts  1.39 us (6%)
    pallas_call x1, Pallas kernels, shards(): pl.pallas_call(functools.partial(kernel, nr, nc, lo), out_shape=(jax.Shap...  20.7 us
    unnamed x2, local copies, waits for them, and re-layouts  1.39 us

profile of v3, /device:TPU:0, one launch (start us, length us, event | category | flops | bytes accessed | tf_op | source)
XLA Modules:
  0.0 25.0 jit_solution(8413946828269976752)
XLA Ops:
  1.3 20.7 %shard_map.58 = (f32[1]{0:T(128)}, f32[16,1024]{1,0:T(8,128)S(1)}, f32[16,1024]{1,0:T(8,128)S(1)}) custom-call(bf16[16,1024]{1,0:T(8,128)(2,1)} %bitcast.7, bf16[16,1024]{1,0:T(8,128)(2,1)} %bitcast.8, f32[1]{0:T(128)S(6)} %copy.9.scale), custom_call_target="tpu_custom_call" | custom-call | tf_op jit(solution)/shard_map/pallas_call | solution.py:176
  21.9 0.7 %copy.6 = f32[16,1,1024]{2,1,0:T(1,128)} copy(f32[16,1,1024]{2,0,1:T(8,128)S(1)} %bitcast.6) | data formatting | bytes 131072
  22.6 0.7 %copy.7 = f32[16,1,1024]{2,1,0:T(1,128)} copy(f32[16,1,1024]{2,0,1:T(8,128)S(1)} %bitcast.5) | data formatting | bytes 131072

commit v4 on v3

--- a/solution.py
+++ b/solution.py
@@ -116,6 +116,12 @@
     row_term = factor * (rexp * jnp.exp(rpeak - row_lse) - jnp.where(eye_t, 2.0, 0.0))
     arrived(cstat, nt - 1, 2)
     col_lse = lse(cstat, nt)
+    lrow[b] = jnp.broadcast_to(jnp.sum(row_lse - 2.0 * diag, axis=1, keepdims=True), (8, 128))
+    lcol[a] = jnp.broadcast_to(jnp.sum(col_lse, axis=1, keepdims=True), (8, 128))
+    for p in tpeers:
+        push(lrow.at[b], lrow.at[b], 6, tdev(p))
+    for p in ipeers:
+        push(lcol.at[a], lcol.at[a], 7, idev(p))
     col_term = factor * (cexp * jnp.exp(cpeak - col_lse))
     delta = (row_term.T + col_term).astype(jnp.bfloat16)
     delta_t = (row_term + col_term.T).astype(jnp.bfloat16)
@@ -131,13 +137,6 @@
 
     idelta[...] = delta.reshape(ni, m, bc)
     tdelta[...] = delta_t.reshape(nt, m, br)
-    lrow[b] = jnp.broadcast_to(jnp.sum(row_lse - 2.0 * diag, axis=1, keepdims=True), (8, 128))
-    lcol[a] = jnp.broadcast_to(jnp.sum(col_lse, axis=1, keepdims=True), (8, 128))
-    for p in tpeers:
-        push(lrow.at[b], lrow.at[b], 6, tdev(p))
-    for p in ipeers:
-        push(lcol.at[a], lcol.at[a], 7, idev(p))
-
     image_total = jnp.dot(idelta[a], texts, preferred_element_type=F32)
     text_total = jnp.dot(tdelta[b], images, preferred_element_type=F32)
     arrived(iin, ni - 1, 5)

time: 25.2 us -> 24.6 us (0.976)
  Pallas kernels: 20.7 us -> 20 us
    pallas_call x1, Pallas kernels: 20.7 us -> 20 us  [shards(): pl.pallas_call(functools.partial(kernel, nr, nc, lo), out_shape=(jax.Shap...]
where the time goes in v4:
time: 24.6 us; the launch traced here: 24.4 us
  Pallas kernels  20 us (81%)
  between operations  2.97 us (12%)
  local copies, waits for them, and re-layouts  1.39 us (6%)
    pallas_call x1, Pallas kernels, shards(): pl.pallas_call(functools.partial(kernel, nr, nc, lo), out_shape=(jax.Shap...  20 us
    unnamed x2, local copies, waits for them, and re-layouts  1.39 us

profile of v4, /device:TPU:0, one launch (start us, length us, event | category | flops | bytes accessed | tf_op | source)
XLA Modules:
  0.0 24.4 jit_solution(10586451120017274212)
XLA Ops:
  1.3 20.0 %shard_map.58 = (f32[1]{0:T(128)}, f32[16,1024]{1,0:T(8,128)S(1)}, f32[16,1024]{1,0:T(8,128)S(1)}) custom-call(bf16[16,1024]{1,0:T(8,128)(2,1)} %bitcast.7, bf16[16,1024]{1,0:T(8,128)(2,1)} %bitcast.8, f32[1]{0:T(128)S(6)} %copy.9.scale), custom_call_target="tpu_custom_call" | custom-call | tf_op jit(solution)/shard_map/pallas_call | solution.py:175
  21.3 0.7 %copy.6 = f32[16,1,1024]{2,1,0:T(1,128)} copy(f32[16,1,1024]{2,0,1:T(8,128)S(1)} %bitcast.6) | data formatting | bytes 131072
  22.0 0.7 %copy.7 = f32[16,1,1024]{2,1,0:T(1,128)} copy(f32[16,1,1024]{2,0,1:T(8,128)S(1)} %bitcast.5) | data formatting | bytes 131072
